TPU v7x, 32 devices: a whole 2x2x4 slice. The times are simulated.
32 devices in a mesh: seq: 8 (over z, x), head: 4 (over y, core).
Axes of the slice: x: 2, y: 2, z: 4, core: 2. Of those that a mesh axis runs over, the one named last changes fastest.
Arguments:
- qkv_pre: bfloat16 [4096, 3, 16, 128], P(('seq', 'head')), may hold values from -10 to 10
- grad_out: bfloat16 [4096, 2048], P(('seq', 'head')), may hold values from -48 to 48
- out_values: bfloat16 [2048, 2048], P('head'), may hold values from -4 to 4
- out_scales: float32 [16, 16], replicated, may hold values from 0.01 to 0.04
- conv_kernel: float32 [31, 3, 16, 128], P(None, None, 'head'), may hold values from -1 to 1
- window: int32 [16], replicated, may hold values from 64 to 96, as said below
- offsets: int32 [8], replicated, may hold values from 0 to 32, as said below
Outputs:
- grad_pre: bfloat16 [4096, 3, 16, 128], P(('seq', 'head'))
Inputs may be any that keep to these rules, and one draw needn't show every extreme that they name: window[h] + offsets[b] <= 128 for every head h and block b; some head has window exactly 96. offsets[b] <= 32 for every block b, with equality in at least one block.
All inputs are finite; a program needn't handle non-finite values.
Results may differ from a plain program's by a relative error of at most 0.005.
The roundings to bfloat16 on the way count: a program that leaves them out, or rounds other values in their place, can miss the bound.
Values may be sent and summed in bfloat16 or wider, within the bound.
No kernel may reach another device: no remote copies, remote signals or barrier semaphores. Data moves between devices by JAX's collectives and lax.ppermute only.
A program may use at most 64 MiB of HBM per device.

v0:
```python
import math
import jax
import jax.numpy as jnp
from jax import lax
from jax.sharding import PartitionSpec as P

KW = 31
MASKB = 512


def shifted(value, axis, by):
    length = lax.axis_size(axis)
    pairs = [(i, i + by) for i in range(length) if 0 <= i + by < length]
    return lax.ppermute(value, axis, pairs)


def causal_conv(series, kernel):
    length = series.shape[0]
    padded = jnp.concatenate(
        [jnp.zeros((KW - 1,) + series.shape[1:], series.dtype), series], axis=0
    )
    summed = jnp.zeros(series.shape, jnp.float32)
    for kernel_tap in range(KW):
        first_row = KW - 1 - kernel_tap
        summed = summed + kernel[kernel_tap] * padded[first_row : first_row + length].astype(
            jnp.float32
        )
    return summed


def transposed_conv(grads, kernel):
    length = grads.shape[0]
    padded = jnp.concatenate([grads, jnp.zeros((KW - 1,) + grads.shape[1:], jnp.float32)], axis=0)
    summed = jnp.zeros(grads.shape, jnp.float32)
    for kernel_tap in range(KW):
        summed = summed + kernel[kernel_tap] * padded[kernel_tap : kernel_tap + length]
    return summed


def dequantize(values, start, out_scales):
    row_count = values.shape[0]
    full_width = values.shape[1]
    block_count = out_scales.shape[0]
    block_size = full_width // out_scales.shape[1]
    column_scales = jnp.repeat(out_scales, block_size, axis=1)
    row_block = (start + lax.iota(jnp.int32, row_count)) // block_size
    picker = (row_block[:, None] == lax.iota(jnp.int32, block_count)[None, :]).astype(jnp.float32)
    scales = jnp.dot(picker, column_scales, precision=lax.Precision.HIGHEST)
    return (values.astype(jnp.float32) * scales).astype(jnp.bfloat16)


def per_device(qkv_pre, grad_out, out_values, out_scales, conv_kernel, window, offsets):
    tok_rows = qkv_pre.shape[0]
    head_count = qkv_pre.shape[2]
    head_dim = qkv_pre.shape[3]
    n_head = lax.axis_size("head")
    local_heads = head_count // n_head
    seq_rows = tok_rows * n_head
    span = seq_rows // 4
    margin = MASKB // 4
    prior = span + margin
    ext_rows = prior + seq_rows
    seq_index = lax.axis_index("seq")
    head_index = lax.axis_index("head")
    inv_scale = 1.0 / math.sqrt(head_dim)
    local_window = lax.dynamic_slice_in_dim(window, head_index * local_heads, local_heads, 0)
    weight = dequantize(out_values, head_index * out_values.shape[0], out_scales)
    grad_heads = lax.dot_general(
        lax.all_gather(grad_out, "head", axis=0, tiled=True),
        weight,
        (((1,), (1,)), ((), ())),
        preferred_element_type=jnp.float32,
    ).astype(jnp.bfloat16)
    grad_heads = grad_heads.reshape(seq_rows, local_heads, head_dim)
    mixed_in = lax.all_to_all(qkv_pre, "head", split_axis=2, concat_axis=0, tiled=True)
    tail_rows = mixed_in[seq_rows - prior :]
    before = shifted(tail_rows, "seq", 1)
    extended = jnp.concatenate([before, mixed_in], axis=0)
    mixed_rows = causal_conv(extended, conv_kernel).astype(jnp.bfloat16)
    query_rows = mixed_rows[prior:, 0]
    key_rows = mixed_rows[:, 1]
    value_rows = mixed_rows[:, 2]
    n_blocks = seq_rows // MASKB
    key_len = span + MASKB
    reach_base = seq_index * n_blocks

    def attend(block_index, totals):
        grad_q, grad_k, grad_v = totals
        q_start = block_index * MASKB
        k_start = margin + q_start
        q_block = lax.dynamic_slice_in_dim(query_rows, q_start, MASKB, 0)
        o_block = lax.dynamic_slice_in_dim(grad_heads, q_start, MASKB, 0)
        k_block = lax.dynamic_slice_in_dim(key_rows, k_start, key_len, 0)
        v_block = lax.dynamic_slice_in_dim(value_rows, k_start, key_len, 0)
        scores = (
            jnp.einsum("qhe,khe->hqk", q_block, k_block, preferred_element_type=jnp.float32)
            * inv_scale
        )
        query_pos = seq_index * seq_rows + q_start + lax.iota(jnp.int32, MASKB)
        key_pos = seq_index * seq_rows - prior + k_start + lax.iota(jnp.int32, key_len)
        distance = query_pos[:, None] - key_pos[None, :]
        reach_now = local_window + lax.dynamic_index_in_dim(
            offsets, reach_base + block_index, 0, keepdims=False
        )
        allowed = ((distance >= 0) & (key_pos[None, :] >= 0))[None] & (
            distance[None] <= reach_now[:, None, None]
        )
        row_top = jnp.max(jnp.where(allowed, scores, -1e30), axis=2, keepdims=True)
        exp_scores = jnp.where(allowed, jnp.exp(scores - row_top), 0.0)
        probs = exp_scores / jnp.sum(exp_scores, axis=2, keepdims=True)
        probs_b = probs.astype(jnp.bfloat16)
        d_prob = jnp.einsum("qhe,khe->hqk", o_block, v_block, preferred_element_type=jnp.float32)
        row_delta = jnp.sum(probs * d_prob, axis=2, keepdims=True)
        d_score = (probs * (d_prob - row_delta) * inv_scale).astype(jnp.bfloat16)
        grad_q_block = jnp.einsum(
            "hqk,khe->qhe", d_score, k_block, preferred_element_type=jnp.float32
        )
        grad_k_block = jnp.einsum(
            "hqk,qhe->khe", d_score, q_block, preferred_element_type=jnp.float32
        )
        grad_v_block = jnp.einsum(
            "hqk,qhe->khe", probs_b, o_block, preferred_element_type=jnp.float32
        )
        grad_q = lax.dynamic_update_slice_in_dim(grad_q, grad_q_block, q_start, 0)
        grad_k = lax.dynamic_update_slice_in_dim(
            grad_k, lax.dynamic_slice_in_dim(grad_k, k_start, key_len, 0) + grad_k_block, k_start, 0
        )
        grad_v = lax.dynamic_update_slice_in_dim(
            grad_v, lax.dynamic_slice_in_dim(grad_v, k_start, key_len, 0) + grad_v_block, k_start, 0
        )
        return (grad_q, grad_k, grad_v)

    start_totals = (
        jnp.zeros((seq_rows, local_heads, head_dim), jnp.float32),
        jnp.zeros((ext_rows, local_heads, head_dim), jnp.float32),
        jnp.zeros((ext_rows, local_heads, head_dim), jnp.float32),
    )
    grad_q, grad_k, grad_v = lax.fori_loop(0, n_blocks, attend, start_totals)
    grad_q_ext = jnp.concatenate(
        [jnp.zeros((prior, local_heads, head_dim), jnp.float32), grad_q], axis=0
    )
    grads = jnp.stack([grad_q_ext, grad_k, grad_v], axis=1)
    spread = transposed_conv(grads, conv_kernel)
    returned = shifted(spread[:prior].astype(jnp.bfloat16), "seq", -1)
    own_rows = spread[prior:]
    tail_sum = own_rows[seq_rows - prior :] + returned.astype(jnp.float32)
    result = jnp.concatenate([own_rows[: seq_rows - prior], tail_sum], axis=0).astype(jnp.bfloat16)
    return lax.all_to_all(result, "head", split_axis=0, concat_axis=2, tiled=True)


def solution(mesh):
    return jax.shard_map(
        per_device,
        mesh=mesh,
        in_specs=(
            P(("seq", "head"), None, None, None),
            P(("seq", "head"), None),
            P("head", None),
            P(),
            P(None, None, "head", None),
            P(),
            P(),
        ),
        out_specs=P(("seq", "head"), None, None, None),
        check_vma=False,
    )
```

profile of v0, /device:TPU:0, one launch (start us, length us, event | category | flops | bytes accessed | tf_op | source)
XLA Modules:
  0.0 214.1 jit_solution(17763769929687273269)
XLA Ops:
  6.5 3.0 %copy.26 = bf16[128,3,16,128]{3,0,1,2:T(8,128)(2,1)} copy(bf16[128,3,16,128]{3,2,1,0:T(8,128)(2,1)} %param.7) | data formatting | bytes 3145728 | tf_op args[0]
  9.5 4.4 %all-to-all-start = ((bf16[128,3,16,128]{3,0,1,2:T(8,128)(2,1)}), bf16[128,3,16,128]{3,0,1,2:T(8,128)(2,1)S(1)}, u32[]{:S(2)}, u32[]{:S(2)}) async-start(bf16[128,3,16,128]{3,0,1,2:T(8,128)(2,1)} %copy.26), calls=%async_computation | async-start | bytes 3145728 | tf_op jit(solution)/shard_map/all_to_all | solution.py:75
  13.9 0.7 all-gather.2.cloned.1.call-update
  14.7 0.7 dynamic_slice.31
  15.3 0.7 dynamic-slice_add_fusion
  16.3 1.1 compare_and_fusion.2
  17.4 22.6 %all-to-all-done = bf16[128,3,16,128]{3,0,1,2:T(8,128)(2,1)S(1)} async-done(((bf16[128,3,16,128]{3,0,1,2:T(8,128)(2,1)}), bf16[128,3,16,128]{3,0,1,2:T(8,128)(2,1)S(1)}, u32[]{:S(2)}, u32[]{:S(2)}) %all-to-all-start) | async-done | bytes 1572896 | tf_op jit(solution)/shard_map/all_to_all | solution.py:75
  40.0 0.2 copy.49
  40.2 4.9 %collective-permute-start = (bf16[256,3,4,128]{3,0,2,1:T(8,128)(2,1)S(1)}, bf16[256,3,4,128]{3,0,2,1:T(8,128)(2,1)S(1)}, u32[]{:S(2)}, u32[]{:S(2)}) collective-permute-start(bf16[256,3,4,128]{3,0,2,1:T(8,128)(2,1)S(1)} %bitcast.129), channel_id=1, source_target_pairs={{0,4},{4,8},{8,12},{12,16},{16,20},{20,24},{24,28},{1,5},{5,9},{9,... | collective-permute-start | bytes 2359304 | tf_op jit(solution)/shard_map/ppermute | solution.py:14
  45.2 1.3 broadcast_subtract_fusion
  46.6 3.3 %multiply_convert_fusion.1 = bf16[512,2048]{1,0:T(8,128)(2,1)} fusion(bf16[512,2048]{1,0:T(8,128)(2,1)S(1)} %copy-done.2, f32[2,8,16,128]{3,2,1,0:T(8,128)S(1)} %bitcast.132, s32[512]{0:T(512)S(1)} %add_select_fusion), kind=kOutput, calls=%fused_computation.16 | convolution fusion | flops 204480512 | bytes 4327424 | tf_op jit(solution)/shard_map/dot_general | solution.py:48
  49.9 11.0 %collective-permute-done = bf16[256,3,4,128]{3,0,2,1:T(8,128)(2,1)S(1)} collective-permute-done((bf16[256,3,4,128]{3,0,2,1:T(8,128)(2,1)S(1)}, bf16[256,3,4,128]{3,0,2,1:T(8,128)(2,1)S(1)}, u32[]{:S(2)}, u32[]{:S(2)}) %collective-permute-start) | collective-permute-done | bytes 786464 | tf_op jit(solution)/shard_map/ppermute | solution.py:14
  60.9 0.9 pad_maximum_fusion.1
  61.9 20.5 %add_convert_fusion = bf16[768,3,4,128]{3,0,2,1:T(8,128)(2,1)} fusion(bf16[798,3,4,128]{3,0,2,1:T(8,128)(2,1)S(1)} %pad_maximum_fusion.1, bf16[512,3,4,128]{3,0,2,1:T(8,128)(2,1)} %bitcast.126, bf16[256,3,4,128]{3,0,2,1:T(8,128)(2,1)S(1)} %collective-permute-done, f32[3,4,128]{2,1,0:T(4,128)S(1)} %get-tuple-element.76, ...), kind=kLoop, calls=%fused_computation.15 | loop fusion | flops 113246208 | bytes 75687936 | tf_op jit(solution)/shard_map/convert_element_type | solution.py:79
  82.4 9.2 %fusion.54 = (f32[4,512]{1,0:T(4,128)}, f32[4,512,640]{2,1,0:T(8,128)}) fusion(s32[512,640]{1,0:T(8,128)} %broadcast_subtract_fusion, s32[4]{0:T(128)S(1)} %dynamic-slice_add_fusion, pred[512,640]{1,0:T(8,128)(4,1)} %compare_and_fusion.2, bf16[768,3,4,128]{3,0,2,1:T(8,128)(2,1)} %add_convert_fusion), kind=kOutput, calls=%fused_computation.105 | convolution fusion | flops 684196480 | bytes 10888192 | tf_op jit(solution)/shard_map/while/body/eval_jaxpr/sub | solution.py:109
  91.6 3.6 %convolution_convert_fusion = bf16[512,512]{1,0:T(8,128)(2,1)S(1)} fusion(bf16[512,2048]{1,0:T(8,128)(2,1)} %multiply_convert_fusion.1, bf16[512,2048]{1,0:T(8,128)(2,1)} %all-gather.2.cloned.1.call-done), kind=kOutput, calls=%fused_computation.40 | convolution fusion | flops 1074003968 | bytes 4718592 | tf_op jit(solution)/shard_map/dot_general | solution.py:68
  95.3 3.3 %fusion.38 = f32[4,512,640]{2,1,0:T(8,128)} fusion(bf16[512,4,128]{0,2,1:T(8,128)(2,1)S(1)} %bitcast.130, bf16[768,3,4,128]{3,0,2,1:T(8,128)(2,1)S(1)} %copy-done.1), kind=kOutput, calls=%fused_computation.43 | convolution fusion | flops 335544320 | bytes 6422528 | tf_op jit(solution)/shard_map/while/body/eval_jaxpr/qhe,khe->hqk/dot_general | solution.py:112
  98.6 17.9 %fusion.33 = f32[512,4,128]{2,0,1:T(8,128)S(1)} fusion(f32[4,512,640]{2,1,0:T(8,128)} %fusion.38, bf16[768,3,4,128]{3,0,2,1:T(8,128)(2,1)S(1)} %copy-done.1, f32[4,512,640]{2,1,0:T(8,128)} %get-tuple-element.79, f32[4,512]{1,0:T(4,128)} %get-tuple-element.78), kind=kOutput, calls=%fused_computation.38 | convolution fusion | flops 344722048 | bytes 22691840 | tf_op jit(solution)/shard_map/while/body/eval_jaxpr/hqk,khe->qhe/dot_general | solution.py:115
  116.5 20.8 %fusion.30 = f32[640,4,128]{2,0,1:T(8,128)} fusion(f32[4,512,640]{2,1,0:T(8,128)} %fusion.38, bf16[768,3,4,128]{3,0,2,1:T(8,128)(2,1)S(1)} %copy-done.1, f32[4,512,640]{2,1,0:T(8,128)} %get-tuple-element.79, f32[4,512]{1,0:T(4,128)} %get-tuple-element.78), kind=kOutput, calls=%fused_computation.37 | convolution fusion | flops 344722048 | bytes 22822912 | tf_op jit(solution)/shard_map/while/body/eval_jaxpr/hqk,qhe->khe/dot_general | solution.py:118
  137.2 4.1 %fusion.27 = f32[640,4,128]{2,0,1:T(8,128)S(1)} fusion(bf16[512,4,128]{0,2,1:T(8,128)(2,1)} %bitcast.131, f32[4,512,640]{2,1,0:T(8,128)} %get-tuple-element.79, f32[4,512]{1,0:T(4,128)} %get-tuple-element.78), kind=kOutput, calls=%fused_computation.36 | convolution fusion | flops 338165760 | bytes 7086080 | tf_op jit(solution)/shard_map/while/body/eval_jaxpr/hqk,qhe->khe/dot_general | solution.py:121
  141.5 0.2 pad_bitcast_fusion
  141.8 0.3 pad_maximum_fusion
  142.2 0.2 copy-done.7
  142.6 18.6 %fusion.52 = (bf16[768,3,4,128]{3,0,2,1:T(8,128)(2,1)S(1)}, f32[768,3,4,128]{3,0,2,1:T(8,128)S(1)}) fusion(f32[3,4,128]{2,1,0:T(4,128)S(1)} %get-tuple-element.76, f32[3,4,128]{2,1,0:T(4,128)S(1)} %get-tuple-element.77, f32[3,4,128]{2,1,0:T(4,128)S(1)} %get-tuple-element.34, f32[3,4,128]{2,1,0:T(4,128)S(1)} %get-tuple-element.35, ...), kind=kLoop, calls=%fused_computation.103 | loop fusion | flops 73138176 | bytes 11986944 | tf_op jit(solution)/shard_map/convert.2
  161.2 0.1 fusion.53
  161.4 1.3 collective-permute-start.1
  162.7 18.7 %collective-permute-done.1 = bf16[256,3,4,128]{3,0,2,1:T(8,128)(2,1)S(1)} collective-permute-done((bf16[256,3,4,128]{3,0,2,1:T(8,128)(2,1)S(1)}, bf16[256,3,4,128]{3,0,2,1:T(8,128)(2,1)S(1)}, u32[]{:S(2)}, u32[]{:S(2)}) %collective-permute-start.1) | collective-permute-done | bytes 786464 | tf_op jit(solution)/shard_map/ppermute | solution.py:14
  181.4 0.2 fusion.26
  181.6 0.1 pad_maximum_fusion.2
  181.7 1.2 copy.34
  182.9 22.7 %all_to_all.36 = bf16[512,3,4,128]{3,2,1,0:T(4,128)(2,1)S(1)} all-to-all(bf16[512,3,4,128]{3,2,1,0:T(4,128)(2,1)S(1)} %copy.34), channel_id=1, replica_groups=mesh['seq'=8,'head'=4] {'head'}, dimensions={0} | all-to-all | bytes 3145728 | tf_op jit(solution)/shard_map/all_to_all | solution.py:148
  205.6 1.7 copy.35
  (82 shorter events, 0.6 us)
Async XLA Ops:
  6.5 8.1 %copy-start.34 = (s32[8]{0:T(128)S(1)}, s32[8]{0:T(128)}, u32[]{:S(2)}) copy-start(s32[8]{0:T(128)} %param.13) | copy-start | bytes 100
  6.5 8.8 %copy-start.33 = (s32[16]{0:T(128)S(1)}, s32[16]{0:T(128)}, u32[]{:S(2)}) copy-start(s32[16]{0:T(128)} %param.12) | copy-start | bytes 196
  6.5 9.6 %copy-start.5 = (f32[31,3,4,128]{3,2,1,0:T(4,128)S(1)}, f32[31,3,4,128]{3,2,1,0:T(4,128)}, u32[]{:S(2)}) copy-start(f32[31,3,4,128]{3,2,1,0:T(4,128)} %param.11) | copy-start | bytes 571396
  9.5 36.9 %copy-start.32 = (f32[16,16]{1,0:T(8,128)S(1)}, f32[16,16]{1,0:T(8,128)}, u32[]{:S(2)}) copy-start(f32[16,16]{1,0:T(8,128)} %param.10) | copy-start | bytes 3076
  9.5 30.4 %all-to-all-start = ((bf16[128,3,16,128]{3,0,1,2:T(8,128)(2,1)}), bf16[128,3,16,128]{3,0,1,2:T(8,128)(2,1)S(1)}, u32[]{:S(2)}, u32[]{:S(2)}) async-start(bf16[128,3,16,128]{3,0,1,2:T(8,128)(2,1)} %copy.26), calls=%async_computation | async-start | bytes 3145728 | tf_op jit(solution)/shard_map/all_to_all | solution.py:75
  13.9 77.7 %all-gather.2.cloned.1.call-start = ((), (), s32[]{:S(2)}) async-start(), calls=%async_computation.2 | async-start | bytes 2621440 | tf_op jit(solution)/shard_map/all_gather | solution.py:69
  16.2 45.6 %copy-start.6 = (f32[3,4,128]{2,1,0:T(4,128)}, f32[3,4,128]{2,1,0:T(4,128)S(1)}, u32[]{:S(2)}) copy-start(f32[3,4,128]{2,1,0:T(4,128)S(1)} %get-tuple-element.53) | copy-start | bytes 18436
  16.2 45.6 %copy-start.8 = (f32[3,4,128]{2,1,0:T(4,128)}, f32[3,4,128]{2,1,0:T(4,128)S(1)}, u32[]{:S(2)}) copy-start(f32[3,4,128]{2,1,0:T(4,128)S(1)} %get-tuple-element.54) | copy-start | bytes 18436
  16.2 45.6 %copy-start.10 = (f32[3,4,128]{2,1,0:T(4,128)}, f32[3,4,128]{2,1,0:T(4,128)S(1)}, u32[]{:S(2)}) copy-start(f32[3,4,128]{2,1,0:T(4,128)S(1)} %get-tuple-element.55) | copy-start | bytes 18436
  16.2 45.6 %copy-start.12 = (f32[3,4,128]{2,1,0:T(4,128)}, f32[3,4,128]{2,1,0:T(4,128)S(1)}, u32[]{:S(2)}) copy-start(f32[3,4,128]{2,1,0:T(4,128)S(1)} %get-tuple-element.56) | copy-start | bytes 18436
  16.2 45.6 %copy-start.14 = (f32[3,4,128]{2,1,0:T(4,128)}, f32[3,4,128]{2,1,0:T(4,128)S(1)}, u32[]{:S(2)}) copy-start(f32[3,4,128]{2,1,0:T(4,128)S(1)} %get-tuple-element.57) | copy-start | bytes 18436
  16.2 45.6 %copy-start.16 = (f32[3,4,128]{2,1,0:T(4,128)}, f32[3,4,128]{2,1,0:T(4,128)S(1)}, u32[]{:S(2)}) copy-start(f32[3,4,128]{2,1,0:T(4,128)S(1)} %get-tuple-element.58) | copy-start | bytes 18436
  16.2 45.6 %copy-start.18 = (f32[3,4,128]{2,1,0:T(4,128)}, f32[3,4,128]{2,1,0:T(4,128)S(1)}, u32[]{:S(2)}) copy-start(f32[3,4,128]{2,1,0:T(4,128)S(1)} %get-tuple-element.59) | copy-start | bytes 18436
  16.2 45.6 %copy-start.20 = (f32[3,4,128]{2,1,0:T(4,128)}, f32[3,4,128]{2,1,0:T(4,128)S(1)}, u32[]{:S(2)}) copy-start(f32[3,4,128]{2,1,0:T(4,128)S(1)} %get-tuple-element.60) | copy-start | bytes 18436
  16.2 45.6 %copy-start.22 = (f32[3,4,128]{2,1,0:T(4,128)}, f32[3,4,128]{2,1,0:T(4,128)S(1)}, u32[]{:S(2)}) copy-start(f32[3,4,128]{2,1,0:T(4,128)S(1)} %get-tuple-element.61) | copy-start | bytes 18436
  16.2 45.6 %copy-start.24 = (f32[3,4,128]{2,1,0:T(4,128)}, f32[3,4,128]{2,1,0:T(4,128)S(1)}, u32[]{:S(2)}) copy-start(f32[3,4,128]{2,1,0:T(4,128)S(1)} %get-tuple-element.62) | copy-start | bytes 18436
  16.3 45.6 %copy-start.26 = (f32[3,4,128]{2,1,0:T(4,128)}, f32[3,4,128]{2,1,0:T(4,128)S(1)}, u32[]{:S(2)}) copy-start(f32[3,4,128]{2,1,0:T(4,128)S(1)} %get-tuple-element.63) | copy-start | bytes 18436
  16.3 45.6 %copy-start.28 = (f32[3,4,128]{2,1,0:T(4,128)}, f32[3,4,128]{2,1,0:T(4,128)S(1)}, u32[]{:S(2)}) copy-start(f32[3,4,128]{2,1,0:T(4,128)S(1)} %get-tuple-element.64) | copy-start | bytes 18436
  16.3 45.6 %copy-start.30 = (f32[3,4,128]{2,1,0:T(4,128)}, f32[3,4,128]{2,1,0:T(4,128)S(1)}, u32[]{:S(2)}) copy-start(f32[3,4,128]{2,1,0:T(4,128)S(1)} %get-tuple-element.65) | copy-start | bytes 18436
  40.0 6.6 %copy-start.2 = (bf16[512,2048]{1,0:T(8,128)(2,1)S(1)}, bf16[512,2048]{1,0:T(8,128)(2,1)}, u32[]{:S(2)}) copy-start(bf16[512,2048]{1,0:T(8,128)(2,1)} %param.9) | copy-start | bytes 6291460
  40.1 21.6 %copy-start = (bf16[128,3,4,4,128]{4,0,2,3,1:T(8,128)(2,1)}, bf16[128,3,4,4,128]{4,0,2,3,1:T(8,128)(2,1)S(1)}, u32[]{:S(2)}) copy-start(bf16[128,3,4,4,128]{4,0,2,3,1:T(8,128)(2,1)S(1)} %copy.49) | copy-start | bytes 4718596
  40.2 20.6 %collective-permute-start = (bf16[256,3,4,128]{3,0,2,1:T(8,128)(2,1)S(1)}, bf16[256,3,4,128]{3,0,2,1:T(8,128)(2,1)S(1)}, u32[]{:S(2)}, u32[]{:S(2)}) collective-permute-start(bf16[256,3,4,128]{3,0,2,1:T(8,128)(2,1)S(1)} %bitcast.129), channel_id=1, source_target_pairs={{0,4},{4,8},{8,12},{12,16},{16,20},{20,24},{24,28},{1,5},{5,9},{9,... | collective-permute-start | bytes 2359304 | tf_op jit(solution)/shard_map/ppermute | solution.py:14
  91.6 3.7 %copy-start.1 = (bf16[768,3,4,128]{3,0,2,1:T(8,128)(2,1)S(1)}, bf16[768,3,4,128]{3,0,2,1:T(8,128)(2,1)}, u32[]{:S(2)}) copy-start(bf16[768,3,4,128]{3,0,2,1:T(8,128)(2,1)} %add_convert_fusion) | copy-start | bytes 7077892
  95.3 3.3 %copy-start.4 = (bf16[512,512]{1,0:T(8,128)(2,1)}, bf16[512,512]{1,0:T(8,128)(2,1)S(1)}, u32[]{:S(2)}) copy-start(bf16[512,512]{1,0:T(8,128)(2,1)S(1)} %convolution_convert_fusion) | copy-start | bytes 1572868
  137.2 4.2 %copy-start.3 = (f32[640,4,128]{2,0,1:T(8,128)S(1)}, f32[640,4,128]{2,0,1:T(8,128)}, u32[]{:S(2)}) copy-start(f32[640,4,128]{2,0,1:T(8,128)} %fusion.30) | copy-start | bytes 3932164
  141.8 0.7 copy-start.21
  141.8 0.7 copy-start.23
  141.8 0.7 copy-start.25
  141.8 0.8 copy-start.27
  141.8 0.8 copy-start.29
  141.8 0.8 copy-start.31
  161.4 20.0 %collective-permute-start.1 = (bf16[256,3,4,128]{3,0,2,1:T(8,128)(2,1)S(1)}, bf16[256,3,4,128]{3,0,2,1:T(8,128)(2,1)S(1)}, u32[]{:S(2)}, u32[]{:S(2)}) collective-permute-start(bf16[256,3,4,128]{3,0,2,1:T(8,128)(2,1)S(1)} %get-tuple-element.30), channel_id=1, source_target_pairs={{4,0},{8,4},{12,8},{16,12},{20,16},{24,20},{28,24},{5,1},{9,5},{13... | collective-permute-start | bytes 2359304 | tf_op jit(solution)/shard_map/ppermute | solution.py:14
  (7 other events, 5.0 us)
Sparse Core Ops, SparseCore 0:
  16.3 30.4 all-gather.1
where the time goes:
time: 215 us; the launch traced here: 214 us
  matrix products  62.2 us (29%)
  waiting for transfers between devices  52.9 us (25%)
  other arithmetic  43.8 us (20%)
  blocking collectives  22.7 us (11%)
  between operations  14 us (7%)
  starting transfers between devices  10.6 us (5%)
  local copies, waits for them, and re-layouts  7.9 us (4%)
    ppermute x2, waiting for transfers between devices, shifted(): return lax.ppermute(value, axis, pairs)  29.6 us
    all_to_all x1, blocking collectives, per_device(): lax.all_to_all(result, 'head', split_axis=0, concat_axis=2, tiled=True)  22.7 us
    all_to_all x1, waiting for transfers between devices, per_device(): lax.all_to_all(qkv_pre, 'head', split_axis=2, concat_axis=0, tiled=True)  22.6 us
    dot_general x1, matrix products, attend(): jnp.einsum('hqk,qhe->khe', d_score, q_block, preferred_element_type=jnp.f...  20.8 us
    convert_element_type x1, other arithmetic, per_device(): mixed_rows = causal_conv(extended, conv_kernel).astype(jnp.bfloat16)  20.5 us
    another operation x2, other arithmetic  18.9 us
    dot_general x1, matrix products, attend(): jnp.einsum('hqk,khe->qhe', d_score, k_block, preferred_element_type=jnp.f...  17.9 us
    sub x1, matrix products, attend(): exp_scores = jnp.where(allowed, jnp.exp(scores - row_top), 0.0)  9.22 us
  transfers between devices with their start and end apart: 4, of which 3 were waited for; matrix products, arithmetic and copies ran while one was open for 18% of the time, Pallas kernels for 0%

commit v1 on v0

--- a/solution.py
+++ b/solution.py
@@ -72,7 +72,18 @@
         preferred_element_type=jnp.float32,
     ).astype(jnp.bfloat16)
     grad_heads = grad_heads.reshape(seq_rows, local_heads, head_dim)
-    mixed_in = lax.all_to_all(qkv_pre, "head", split_axis=2, concat_axis=0, tiled=True)
+    reply = lax.axis_size("head")
+    reached, front = (reply, lax.axis_index("head"))
+    z1 = qkv_pre.shape[2] // reached
+    step_out = jnp.roll(qkv_pre, -front * z1, 2)
+    aux = lax.slice_in_dim(step_out, 0, z1, axis=2)
+    inbox = [aux]
+    for pp in range(1, reached):
+        fresh = lax.slice_in_dim(step_out, pp * z1, (pp + 1) * z1, axis=2)
+        y_new = lax.ppermute(fresh, "head", perm=[(p, (p + pp) % reached) for p in range(reached)])
+        inbox.append(y_new)
+    x_now = jnp.concatenate(inbox[::-1], axis=0)
+    mixed_in = jnp.roll(x_now, (front + 1) * inbox[0].shape[0], 0)
     tail_rows = mixed_in[seq_rows - prior :]
     before = shifted(tail_rows, "seq", 1)
     extended = jnp.concatenate([before, mixed_in], axis=0)

time: 215 us -> 214 us (level)
  local copies, waits for them, and re-layouts: 7.9 us -> 12.2 us
  waiting for transfers between devices: 52.9 us -> 49 us
  starting transfers between devices: 10.6 us -> 7.78 us
    all_to_all x1 -> x0, waiting for transfers between devices: 22.6 us -> none  [per_device(): lax.all_to_all(qkv_pre, 'head', split_axis=2, concat_axis=0, tiled=True)]
    ppermute x0 -> x3, waiting for transfers between devices: none -> 19.6 us  [per_device(): lax.ppermute(fresh, 'head', perm=[(p, (p + pp) % reached) for p in range(...]
    all_to_all x1 -> x0, starting transfers between devices: 4.37 us -> none  [per_device(): lax.all_to_all(qkv_pre, 'head', split_axis=2, concat_axis=0, tiled=True)]
    ppermute x0 -> x3, starting transfers between devices: none -> 3.2 us  [per_device(): lax.ppermute(fresh, 'head', perm=[(p, (p + pp) % reached) for p in range(...]
  transfers between devices with their start and end apart: 4 -> 6, of which waited for: 3 -> 4; matrix products, arithmetic and copies ran while one was open for 18% -> 20% of each run, Pallas kernels for 0% -> 0%
where the time goes in v1:
time: 214 us; the launch traced here: 213 us
  matrix products  62.4 us (29%)
  waiting for transfers between devices  49 us (23%)
  other arithmetic  45 us (21%)
  blocking collectives  22.5 us (11%)
  between operations  14.3 us (7%)
  local copies, waits for them, and re-layouts  12.2 us (6%)
  starting transfers between devices  7.78 us (4%)
    ppermute x2, waiting for transfers between devices, shifted(): return lax.ppermute(value, axis, pairs)  29.3 us
    all_to_all x1, blocking collectives, per_device(): lax.all_to_all(result, 'head', split_axis=0, concat_axis=2, tiled=True)  22.5 us
    dot_general x1, matrix products, attend(): jnp.einsum('hqk,qhe->khe', d_score, q_block, preferred_element_type=jnp.f...  20.9 us
    convert_element_type x1, other arithmetic, per_device(): mixed_rows = causal_conv(extended, conv_kernel).astype(jnp.bfloat16)  20.5 us
    ppermute x3, waiting for transfers between devices, per_device(): lax.ppermute(fresh, 'head', perm=[(p, (p + pp) % reached) for p in range(...  19.6 us
    another operation x2, other arithmetic  18.9 us
    dot_general x1, matrix products, attend(): jnp.einsum('hqk,khe->qhe', d_score, k_block, preferred_element_type=jnp.f...  18 us
    sub x1, matrix products, attend(): exp_scores = jnp.where(allowed, jnp.exp(scores - row_top), 0.0)  9.09 us
  transfers between devices with their start and end apart: 6, of which 4 were waited for; matrix products, arithmetic and copies ran while one was open for 20% of the time, Pallas kernels for 0%

profile of v1, /device:TPU:0, one launch (start us, length us, event | category | flops | bytes accessed | tf_op | source)
XLA Modules:
  0.0 213.1 jit_solution(12444466828085359153)
XLA Ops:
  6.5 1.8 copy.17
  8.4 0.6 fusion.26
  9.0 0.9 fusion.55
  9.8 2.4 %collective-permute-start = (bf16[128,3,4,128]{3,0,2,1:T(8,128)(2,1)}, bf16[128,3,4,128]{3,0,2,1:T(8,128)(2,1)S(1)}, u32[]{:S(2)}, u32[]{:S(2)}) collective-permute-start(bf16[128,3,4,128]{3,0,2,1:T(8,128)(2,1)} %get-tuple-element.33), channel_id=1, source_target_pairs={{0,3},{1,0},{2,1},{3,2},{4,7},{5,4},{6,5},{7,6},{8,11},{9,8},{10,9... | collective-permute-start | bytes 1179656 | tf_op jit(solution)/shard_map/ppermute | solution.py:83
  12.2 0.6 collective-permute-start.1
  13.1 1.1 compare_and_fusion.2
  14.2 1.5 slice_bitcast_fusion.46
  15.7 1.5 slice_bitcast_fusion.45
  17.3 1.4 dynamic_slice.41
  18.7 3.4 %collective-permute-done = bf16[128,3,4,128]{3,0,2,1:T(8,128)(2,1)S(1)} collective-permute-done((bf16[128,3,4,128]{3,0,2,1:T(8,128)(2,1)}, bf16[128,3,4,128]{3,0,2,1:T(8,128)(2,1)S(1)}, u32[]{:S(2)}, u32[]{:S(2)}) %collective-permute-start) | collective-permute-done | bytes 393248 | tf_op jit(solution)/shard_map/ppermute | solution.py:83
  22.1 16.3 %collective-permute-done.1 = bf16[128,3,4,128]{3,0,2,1:T(8,128)(2,1)S(1)} collective-permute-done((bf16[128,3,4,128]{3,0,2,1:T(8,128)(2,1)S(1)}, bf16[128,3,4,128]{3,0,2,1:T(8,128)(2,1)S(1)}, u32[]{:S(2)}, u32[]{:S(2)}) %collective-permute-start.1) | collective-permute-done | bytes 393248 | tf_op jit(solution)/shard_map/ppermute | solution.py:83
  39.0 3.3 %collective-permute-start.3 = (bf16[256,3,4,128]{3,0,2,1:T(8,128)(2,1)S(1)}, bf16[256,3,4,128]{3,0,2,1:T(8,128)(2,1)S(1)}, u32[]{:S(2)}, u32[]{:S(2)}) collective-permute-start(bf16[256,3,4,128]{3,0,2,1:T(8,128)(2,1)S(1)} %constant_dynamic-slice_fusion.1), channel_id=1, source_target_pairs={{0,4},{4,8},{8,12},{12,16},{16,20},{20,24},{24,28},{1,5},{5,9},{9,... | collective-permute-start | bytes 2359304 | tf_op jit(solution)/shard_map/ppermute | solution.py:14
  42.3 1.3 dynamic-slice_add_fusion
  43.6 1.3 broadcast_subtract_fusion
  45.0 3.4 %multiply_convert_fusion.1 = bf16[512,2048]{1,0:T(8,128)(2,1)} fusion(bf16[512,2048]{1,0:T(8,128)(2,1)S(1)} %copy-done.2, f32[2,8,16,128]{3,2,1,0:T(8,128)S(1)} %bitcast.120, s32[512]{0:T(512)S(1)} %add_select_fusion), kind=kOutput, calls=%fused_computation.16 | convolution fusion | flops 204480512 | bytes 4327424 | tf_op jit(solution)/shard_map/dot_general | solution.py:48
  48.6 0.4 constant_dynamic-slice_fusion
  49.1 9.8 %collective-permute-done.3 = bf16[256,3,4,128]{3,0,2,1:T(8,128)(2,1)S(1)} collective-permute-done((bf16[256,3,4,128]{3,0,2,1:T(8,128)(2,1)S(1)}, bf16[256,3,4,128]{3,0,2,1:T(8,128)(2,1)S(1)}, u32[]{:S(2)}, u32[]{:S(2)}) %collective-permute-start.3) | collective-permute-done | bytes 786464 | tf_op jit(solution)/shard_map/ppermute | solution.py:14
  58.9 0.9 pad_maximum_fusion.1
  60.1 20.5 %add_convert_fusion = bf16[768,3,4,128]{3,0,2,1:T(8,128)(2,1)} fusion(bf16[798,3,4,128]{3,0,2,1:T(8,128)(2,1)S(1)} %pad_maximum_fusion.1, bf16[512,3,4,128]{3,0,2,1:T(8,128)(2,1)} %copy-done, bf16[256,3,4,128]{3,0,2,1:T(8,128)(2,1)S(1)} %collective-permute-done.3, f32[3,4,128]{2,1,0:T(4,128)S(1)} %copy-done.13, f32[3,4,128]{2,1,0:T(4,128)S(1)} %copy-done.14, ...), kind=kLoop, calls=%fused_computation.15 | loop fusion | flops 113246208 | bytes 75687936 | tf_op jit(solution)/shard_map/convert_element_type | solution.py:90
  80.6 9.1 %fusion.56 = (f32[4,512]{1,0:T(4,128)}, f32[4,512,640]{2,1,0:T(8,128)}) fusion(s32[512,640]{1,0:T(8,128)} %broadcast_subtract_fusion, s32[4]{0:T(128)S(1)} %dynamic-slice_add_fusion, pred[512,640]{1,0:T(8,128)(4,1)} %compare_and_fusion.2, bf16[768,3,4,128]{3,0,2,1:T(8,128)(2,1)} %add_convert_fusion), kind=kOutput, calls=%fused_computation.118 | convolution fusion | flops 684196480 | bytes 10888192 | tf_op jit(solution)/shard_map/while/body/eval_jaxpr/sub | solution.py:120
  89.7 3.7 %convolution_convert_fusion = bf16[512,512]{1,0:T(8,128)(2,1)S(1)} fusion(bf16[512,2048]{1,0:T(8,128)(2,1)} %multiply_convert_fusion.1, bf16[512,2048]{1,0:T(8,128)(2,1)} %all-gather.2.cloned.1.call-done), kind=kOutput, calls=%fused_computation.43 | convolution fusion | flops 1074003968 | bytes 4718592 | tf_op jit(solution)/shard_map/dot_general | solution.py:68
  93.4 3.3 %fusion.39 = f32[4,512,640]{2,1,0:T(8,128)} fusion(bf16[512,4,128]{0,2,1:T(8,128)(2,1)S(1)} %bitcast.118, bf16[768,3,4,128]{3,0,2,1:T(8,128)(2,1)S(1)} %copy-done.1), kind=kOutput, calls=%fused_computation.46 | convolution fusion | flops 335544320 | bytes 6422528 | tf_op jit(solution)/shard_map/while/body/eval_jaxpr/qhe,khe->hqk/dot_general | solution.py:123
  96.6 18.0 %fusion.34 = f32[512,4,128]{2,0,1:T(8,128)S(1)} fusion(f32[4,512,640]{2,1,0:T(8,128)} %fusion.39, bf16[768,3,4,128]{3,0,2,1:T(8,128)(2,1)S(1)} %copy-done.1, f32[4,512,640]{2,1,0:T(8,128)} %get-tuple-element.80, f32[4,512]{1,0:T(4,128)} %get-tuple-element.79), kind=kOutput, calls=%fused_computation.41 | convolution fusion | flops 344722048 | bytes 22691840 | tf_op jit(solution)/shard_map/while/body/eval_jaxpr/hqk,khe->qhe/dot_general | solution.py:126
  114.6 20.9 %fusion.31 = f32[640,4,128]{2,0,1:T(8,128)} fusion(f32[4,512,640]{2,1,0:T(8,128)} %fusion.39, bf16[768,3,4,128]{3,0,2,1:T(8,128)(2,1)S(1)} %copy-done.1, f32[4,512,640]{2,1,0:T(8,128)} %get-tuple-element.80, f32[4,512]{1,0:T(4,128)} %get-tuple-element.79), kind=kOutput, calls=%fused_computation.40 | convolution fusion | flops 344722048 | bytes 22822912 | tf_op jit(solution)/shard_map/while/body/eval_jaxpr/hqk,qhe->khe/dot_general | solution.py:129
  135.5 4.1 %fusion.28 = f32[640,4,128]{2,0,1:T(8,128)S(1)} fusion(bf16[512,4,128]{0,2,1:T(8,128)(2,1)} %bitcast.119, f32[4,512,640]{2,1,0:T(8,128)} %get-tuple-element.80, f32[4,512]{1,0:T(4,128)} %get-tuple-element.79), kind=kOutput, calls=%fused_computation.39 | convolution fusion | flops 338165760 | bytes 7086080 | tf_op jit(solution)/shard_map/while/body/eval_jaxpr/hqk,qhe->khe/dot_general | solution.py:132
  140.1 0.3 pad_maximum_fusion
  140.9 18.6 %fusion.53 = (bf16[768,3,4,128]{3,0,2,1:T(8,128)(2,1)S(1)}, f32[768,3,4,128]{3,0,2,1:T(8,128)S(1)}) fusion(f32[3,4,128]{2,1,0:T(4,128)S(1)} %copy-done.13, f32[3,4,128]{2,1,0:T(4,128)S(1)} %copy-done.14, f32[3,4,128]{2,1,0:T(4,128)S(1)} %copy-done.16, f32[3,4,128]{2,1,0:T(4,128)S(1)} %copy-done.17, f32[3,4,128]{2,1,0:T(4,128)S(1)} %copy-done.18, ...), kind=kLoop, calls=%fused_computation.115 | loop fusion | flops 73138176 | bytes 11986944 | tf_op jit(solution)/shard_map/convert.2
  159.7 1.3 collective-permute-start.4
  161.0 19.5 %collective-permute-done.4 = bf16[256,3,4,128]{3,0,2,1:T(8,128)(2,1)S(1)} collective-permute-done((bf16[256,3,4,128]{3,0,2,1:T(8,128)(2,1)S(1)}, bf16[256,3,4,128]{3,0,2,1:T(8,128)(2,1)S(1)}, u32[]{:S(2)}, u32[]{:S(2)}) %collective-permute-start.4) | collective-permute-done | bytes 786464 | tf_op jit(solution)/shard_map/ppermute | solution.py:14
  180.9 1.2 copy.25
  182.1 22.5 %all_to_all.18 = bf16[512,3,4,128]{3,2,1,0:T(4,128)(2,1)S(1)} all-to-all(bf16[512,3,4,128]{3,2,1,0:T(4,128)(2,1)S(1)} %copy.25), channel_id=1, replica_groups=mesh['seq'=8,'head'=4] {'head'}, dimensions={0} | all-to-all | bytes 3145728 | tf_op jit(solution)/shard_map/all_to_all | solution.py:159
  204.6 1.7 copy.26
  (130 shorter events, 2.4 us)
Async XLA Ops:
  6.5 83.1 %all-gather.2.cloned.1.call-start = ((), (), s32[]{:S(2)}) async-start(), calls=%async_computation.1 | async-start | bytes 2621440 | tf_op jit(solution)/shard_map/all_gather | solution.py:69
  9.8 12.2 %collective-permute-start = (bf16[128,3,4,128]{3,0,2,1:T(8,128)(2,1)}, bf16[128,3,4,128]{3,0,2,1:T(8,128)(2,1)S(1)}, u32[]{:S(2)}, u32[]{:S(2)}) collective-permute-start(bf16[128,3,4,128]{3,0,2,1:T(8,128)(2,1)} %get-tuple-element.33), channel_id=1, source_target_pairs={{0,3},{1,0},{2,1},{3,2},{4,7},{5,4},{6,5},{7,6},{8,11},{9,8},{10,9... | collective-permute-start | bytes 1179656 | tf_op jit(solution)/shard_map/ppermute | solution.py:83
  12.2 26.1 %collective-permute-start.1 = (bf16[128,3,4,128]{3,0,2,1:T(8,128)(2,1)S(1)}, bf16[128,3,4,128]{3,0,2,1:T(8,128)(2,1)S(1)}, u32[]{:S(2)}, u32[]{:S(2)}) collective-permute-start(bf16[128,3,4,128]{3,0,2,1:T(8,128)(2,1)S(1)} %get-tuple-element.32), channel_id=1, source_target_pairs={{0,2},{1,3},{2,0},{3,1},{4,6},{5,7},{6,4},{7,5},{8,10},{9,11},{10,... | collective-permute-start | bytes 1179656 | tf_op jit(solution)/shard_map/ppermute | solution.py:83
  12.8 25.6 %collective-permute-start.2 = (bf16[128,3,4,128]{3,0,2,1:T(8,128)(2,1)S(1)}, bf16[128,3,4,128]{3,0,2,1:T(8,128)(2,1)S(1)}, u32[]{:S(2)}, u32[]{:S(2)}) collective-permute-start(bf16[128,3,4,128]{3,0,2,1:T(8,128)(2,1)S(1)} %get-tuple-element.31), channel_id=1, source_target_pairs={{0,1},{1,2},{2,3},{3,0},{4,5},{5,6},{6,7},{7,4},{8,9},{9,10},{10,1... | collective-permute-start | bytes 1179656 | tf_op jit(solution)/shard_map/ppermute | solution.py:83
  17.3 26.4 %copy-start.48 = (s32[640]{0:T(1024)S(1)}, s32[640]{0:T(1024)}, u32[]{:S(2)}) copy-start(s32[640]{0:T(1024)} %copy-done.47) | copy-start | bytes 7684
  17.3 26.4 %copy-start.50 = (s32[512]{0:T(512)S(1)}, s32[512]{0:T(512)}, u32[]{:S(2)}) copy-start(s32[512]{0:T(512)} %copy-done.49) | copy-start | bytes 6148
  17.3 27.6 %copy-start.51 = (f32[16,16]{1,0:T(8,128)S(1)}, f32[16,16]{1,0:T(8,128)}, u32[]{:S(2)}) copy-start(f32[16,16]{1,0:T(8,128)} %param.10) | copy-start | bytes 3076
  17.3 27.7 %copy-start.2 = (bf16[512,2048]{1,0:T(8,128)(2,1)S(1)}, bf16[512,2048]{1,0:T(8,128)(2,1)}, u32[]{:S(2)}) copy-start(bf16[512,2048]{1,0:T(8,128)(2,1)} %param.9) | copy-start | bytes 6291460
  39.0 19.9 %collective-permute-start.3 = (bf16[256,3,4,128]{3,0,2,1:T(8,128)(2,1)S(1)}, bf16[256,3,4,128]{3,0,2,1:T(8,128)(2,1)S(1)}, u32[]{:S(2)}, u32[]{:S(2)}) collective-permute-start(bf16[256,3,4,128]{3,0,2,1:T(8,128)(2,1)S(1)} %constant_dynamic-slice_fusion.1), channel_id=1, source_target_pairs={{0,4},{4,8},{8,12},{12,16},{16,20},{20,24},{24,28},{1,5},{5,9},{9,... | collective-permute-start | bytes 2359304 | tf_op jit(solution)/shard_map/ppermute | solution.py:14
  48.4 11.4 %copy-start.9 = (f32[3,4,128]{2,1,0:T(4,128)S(1)}, f32[3,4,128]{2,1,0:T(4,128)}, u32[]{:S(2)}) copy-start(f32[3,4,128]{2,1,0:T(4,128)} %get-tuple-element.73) | copy-start | bytes 18436
  48.4 11.4 %copy-start.10 = (f32[3,4,128]{2,1,0:T(4,128)S(1)}, f32[3,4,128]{2,1,0:T(4,128)}, u32[]{:S(2)}) copy-start(f32[3,4,128]{2,1,0:T(4,128)} %get-tuple-element.74) | copy-start | bytes 18436
  48.4 11.4 %copy-start.11 = (f32[3,4,128]{2,1,0:T(4,128)S(1)}, f32[3,4,128]{2,1,0:T(4,128)}, u32[]{:S(2)}) copy-start(f32[3,4,128]{2,1,0:T(4,128)} %get-tuple-element.75) | copy-start | bytes 18436
  48.4 11.4 %copy-start.12 = (f32[3,4,128]{2,1,0:T(4,128)S(1)}, f32[3,4,128]{2,1,0:T(4,128)}, u32[]{:S(2)}) copy-start(f32[3,4,128]{2,1,0:T(4,128)} %get-tuple-element.76) | copy-start | bytes 18436
  48.4 11.4 %copy-start.13 = (f32[3,4,128]{2,1,0:T(4,128)S(1)}, f32[3,4,128]{2,1,0:T(4,128)}, u32[]{:S(2)}) copy-start(f32[3,4,128]{2,1,0:T(4,128)} %get-tuple-element.77) | copy-start | bytes 18436
  48.4 11.4 %copy-start.14 = (f32[3,4,128]{2,1,0:T(4,128)S(1)}, f32[3,4,128]{2,1,0:T(4,128)}, u32[]{:S(2)}) copy-start(f32[3,4,128]{2,1,0:T(4,128)} %get-tuple-element.78) | copy-start | bytes 18436
  48.4 11.4 %copy-start.15 = (f32[3,4,128]{2,1,0:T(4,128)S(1)}, f32[3,4,128]{2,1,0:T(4,128)}, u32[]{:S(2)}) copy-start(f32[3,4,128]{2,1,0:T(4,128)} %get-tuple-element.34) | copy-start | bytes 18436
  48.5 11.4 %copy-start.16 = (f32[3,4,128]{2,1,0:T(4,128)S(1)}, f32[3,4,128]{2,1,0:T(4,128)}, u32[]{:S(2)}) copy-start(f32[3,4,128]{2,1,0:T(4,128)} %get-tuple-element.35) | copy-start | bytes 18436
  48.5 11.4 %copy-start.17 = (f32[3,4,128]{2,1,0:T(4,128)S(1)}, f32[3,4,128]{2,1,0:T(4,128)}, u32[]{:S(2)}) copy-start(f32[3,4,128]{2,1,0:T(4,128)} %get-tuple-element.48) | copy-start | bytes 18436
  48.5 11.4 %copy-start.18 = (f32[3,4,128]{2,1,0:T(4,128)S(1)}, f32[3,4,128]{2,1,0:T(4,128)}, u32[]{:S(2)}) copy-start(f32[3,4,128]{2,1,0:T(4,128)} %get-tuple-element.50) | copy-start | bytes 18436
  48.5 11.4 %copy-start.19 = (f32[3,4,128]{2,1,0:T(4,128)S(1)}, f32[3,4,128]{2,1,0:T(4,128)}, u32[]{:S(2)}) copy-start(f32[3,4,128]{2,1,0:T(4,128)} %get-tuple-element.52) | copy-start | bytes 18436
  48.5 11.4 %copy-start.20 = (f32[3,4,128]{2,1,0:T(4,128)S(1)}, f32[3,4,128]{2,1,0:T(4,128)}, u32[]{:S(2)}) copy-start(f32[3,4,128]{2,1,0:T(4,128)} %get-tuple-element.53) | copy-start | bytes 18436
  48.5 11.4 %copy-start.21 = (f32[3,4,128]{2,1,0:T(4,128)S(1)}, f32[3,4,128]{2,1,0:T(4,128)}, u32[]{:S(2)}) copy-start(f32[3,4,128]{2,1,0:T(4,128)} %get-tuple-element.54) | copy-start | bytes 18436
  48.5 11.4 %copy-start.23 = (f32[3,4,128]{2,1,0:T(4,128)S(1)}, f32[3,4,128]{2,1,0:T(4,128)}, u32[]{:S(2)}) copy-start(f32[3,4,128]{2,1,0:T(4,128)} %get-tuple-element.55) | copy-start | bytes 18436
  48.5 11.4 %copy-start.25 = (f32[3,4,128]{2,1,0:T(4,128)S(1)}, f32[3,4,128]{2,1,0:T(4,128)}, u32[]{:S(2)}) copy-start(f32[3,4,128]{2,1,0:T(4,128)} %get-tuple-element.56) | copy-start | bytes 18436
  48.5 11.4 %copy-start.27 = (f32[3,4,128]{2,1,0:T(4,128)S(1)}, f32[3,4,128]{2,1,0:T(4,128)}, u32[]{:S(2)}) copy-start(f32[3,4,128]{2,1,0:T(4,128)} %get-tuple-element.57) | copy-start | bytes 18436
  48.5 11.4 %copy-start.29 = (f32[3,4,128]{2,1,0:T(4,128)S(1)}, f32[3,4,128]{2,1,0:T(4,128)}, u32[]{:S(2)}) copy-start(f32[3,4,128]{2,1,0:T(4,128)} %get-tuple-element.58) | copy-start | bytes 18436
  48.5 11.4 %copy-start.31 = (f32[3,4,128]{2,1,0:T(4,128)S(1)}, f32[3,4,128]{2,1,0:T(4,128)}, u32[]{:S(2)}) copy-start(f32[3,4,128]{2,1,0:T(4,128)} %get-tuple-element.59) | copy-start | bytes 18436
  48.6 11.4 %copy-start.33 = (f32[3,4,128]{2,1,0:T(4,128)S(1)}, f32[3,4,128]{2,1,0:T(4,128)}, u32[]{:S(2)}) copy-start(f32[3,4,128]{2,1,0:T(4,128)} %get-tuple-element.60) | copy-start | bytes 18436
  48.6 11.4 %copy-start.35 = (f32[3,4,128]{2,1,0:T(4,128)S(1)}, f32[3,4,128]{2,1,0:T(4,128)}, u32[]{:S(2)}) copy-start(f32[3,4,128]{2,1,0:T(4,128)} %get-tuple-element.61) | copy-start | bytes 18436
  48.6 11.4 %copy-start.37 = (f32[3,4,128]{2,1,0:T(4,128)S(1)}, f32[3,4,128]{2,1,0:T(4,128)}, u32[]{:S(2)}) copy-start(f32[3,4,128]{2,1,0:T(4,128)} %get-tuple-element.62) | copy-start | bytes 18436
  48.6 11.4 %copy-start.39 = (f32[3,4,128]{2,1,0:T(4,128)S(1)}, f32[3,4,128]{2,1,0:T(4,128)}, u32[]{:S(2)}) copy-start(f32[3,4,128]{2,1,0:T(4,128)} %get-tuple-element.63) | copy-start | bytes 18436
  159.7 20.8 %collective-permute-start.4 = (bf16[256,3,4,128]{3,0,2,1:T(8,128)(2,1)S(1)}, bf16[256,3,4,128]{3,0,2,1:T(8,128)(2,1)S(1)}, u32[]{:S(2)}, u32[]{:S(2)}) collective-permute-start(bf16[256,3,4,128]{3,0,2,1:T(8,128)(2,1)S(1)} %get-tuple-element.30), channel_id=1, source_target_pairs={{4,0},{8,4},{12,8},{16,12},{20,16},{24,20},{28,24},{5,1},{9,5},{13... | collective-permute-start | bytes 2359304 | tf_op jit(solution)/shard_map/ppermute | solution.py:14
  (26 other events, 112.7 us)
Sparse Core Ops, SparseCore 0:
  13.2 30.5 all-gather.1
